TPU v7x, 32 devices: a whole 2x2x4 slice. The times are simulated.
32 devices in a mesh: bl: 8 (over z, y), comp: 4 (over x, core).
Axes of the slice: x: 2, y: 2, z: 4, core: 2. Of those that a mesh axis runs over, the one named last changes fastest.
Arguments:
- baseline_uvw: float32 [3, 8192], P(None, ('bl', 'comp')), may hold values from -96 to 96
- antenna_pair: int32 [2, 8192], P(None, ('bl', 'comp')), may hold values from 0 to 511, as said below
- row_count: int32 [32], P(('bl', 'comp')), may hold values from 32 to 256, as said below
- comp_position: float32 [2, 8192], P(None, 'comp'), may hold values from -0.3 to 0.3
- comp_flux: float32 [4, 16, 8192], P(None, None, 'comp'), may hold values from -0.0625 to 0.0625
- gain: float32 [512, 256], P(('bl', 'comp')), may hold values from -4.2 to 4.2
- antenna_owner: int32 [512], replicated, may hold values from 0 to 31, as said below
- observed: float32 [8192, 128], P(('bl', 'comp')), may hold values from -6 to 6
Outputs:
- residual: float32 [8192, 128], P(('bl', 'comp'))
- normal_blocks: float32 [512, 384], P(('bl', 'comp'))
Inputs may be any that keep to these rules, and one draw needn't show every extreme that they name: `antenna_pair`: the two antennas of a row differ. `row_count`: a multiple of 32; slots at or beyond it on that device are padding; some device is full. `antenna_owner`: each of the 32 owners holds exactly 16 antennas.
All inputs are finite; a program needn't handle non-finite values.
Results may differ from a plain program's by a relative error of at most 0.0003.
Values sent between devices are 32-bit elements; how exact they have to be, the bound alone decides.
No kernel may reach another device: no remote copies, remote signals or barrier semaphores. Data moves between devices by JAX's collectives and lax.ppermute only.
A program may use at most 448 MiB of HBM per device.

v0:
```python
import jax
import jax.numpy as jnp
from jax import lax
from jax.experimental import pallas as pl
from jax.experimental.pallas import tpu as pltpu
from jax.sharding import PartitionSpec as P

CHANNELS = 16
TIMES = 4
GROUP = 4
LANES = 256
DEPTH = 256
STRIP = 16
F32 = jnp.float32
BF16 = jnp.bfloat16

SIN = [4 * v for v in (4.4428679030304945, -7.307443421264523, 3.5947880783696866, -0.7843740306721513)]
COS = [4 * v for v in (1.4142040804669556, -6.977642056688728, 5.71523839383031, -1.7283486597599615)]
CENTRES = (1 + 3.5 / 32, 1 + 11.5 / 32)
HALF_STEP = 1 / 64
TERMS = ((0, 0), (0, 1), (0, 2), (1, 0), (1, 1), (2, 0))


def pieces(x, count):
    out = []
    for _ in range(count):
        piece = lax.reduce_precision(x, 8, 7)
        out.append(piece.astype(BF16))
        x = x - piece
    return out


def turn(x):
    r = x - jnp.round(x)
    q = r * r
    s = (((SIN[3] * q + SIN[2]) * q + SIN[1]) * q + SIN[0]) * r
    c = ((COS[3] * q + COS[2]) * q + COS[1]) * q + COS[0]
    return 16.0 - s * s, s * c


def factors(t, put):
    for a, centre in enumerate(CENTRES):
        pair = turn(t * centre)
        yield
        for m, v in enumerate(pair):
            hi = jnp.round(v)
            for n, part in enumerate((hi, v - hi, v)):
                put(6 * a + 3 * m + n, part.astype(BF16))
        yield
    c, s = turn(t * HALF_STEP)
    yield
    twice = (c * c) * (4.0 / 256.0) - 2.0
    cs, ss = [c, (twice - 1.0) * c], [s, (twice + 1.0) * s]
    for k in range(4):
        if k > 1:
            cs.append(twice * cs[-1] - cs[-2])
            ss.append(twice * ss[-1] - ss[-2])
        for m, v in enumerate((cs[k], ss[k])):
            hi = jnp.round(v)
            put(12 + 4 * k + 2 * m, hi.astype(BF16))
            put(13 + 4 * k + 2 * m, (v - hi).astype(BF16))
        yield


FACTORS = 28
PIECES = 9


def group_rows(info_ref, heads):
    me = info_ref[0]
    counts = [jnp.max(head[5:6, 0:128]).astype(jnp.int32) for head in heads]
    starts = [
        sum(jnp.where((me ^ c) < (me ^ b), counts[c], 0) for c in range(GROUP)) for b in range(GROUP)
    ]
    return starts, counts, sum(counts)


def place(ref, value, start, count):
    block, off = lax.div(start, LANES), lax.rem(start, LANES)
    lane = lax.broadcasted_iota(jnp.int32, value.shape, 1)
    turned = pltpu.roll(value, off, 1)
    ref[block] = jnp.where((lane >= off) & (lane < off + count), turned, ref[block])
    ref[block + 1] = jnp.where((lane < off) & (lane + LANES < off + count), turned, ref[block + 1])


def taken(ref, start, count):
    block, off = lax.div(start, LANES), lax.rem(start, LANES)
    back = lax.rem(LANES - off, LANES)
    first, second = pltpu.roll(ref[block], back, 1), pltpu.roll(ref[block + 1], back, 1)
    lane = lax.broadcasted_iota(jnp.int32, first.shape, 1)
    return jnp.where(lane < count, jnp.where(lane < LANES - off, first, second), 0.0)


def predict_kernel(blocks, info_ref, h0, h1, h2, h3, l_ref, tab_ref, o_ref, fa, fb, tt, ta, tb, acc, rows_ref, u_ref):
    starts, counts, live = group_rows(info_ref, (h0, h1, h2, h3))
    total = lax.div(live + LANES - 1, LANES) * blocks
    rows_ref[...] = jnp.zeros_like(rows_ref)
    for b, head in enumerate((h0, h1, h2, h3)):
        place(rows_ref, head[0:8], starts[b], counts[b])
    for row in range(u_ref.shape[0]):
        parts, rest = [], rows_ref[row]
        for _ in range(3):
            part = rest.astype(BF16).astype(F32)
            parts.append(part)
            rest = rest - part
        u_ref[row] = jnp.concatenate([parts[i] for i, _ in TERMS], axis=0).astype(BF16)

    def begin(index, table):
        index = jnp.minimum(index, total - 1)
        row, block = lax.div(index, blocks), lax.rem(index, blocks)
        comps = pl.ds(pl.multiple_of(block * DEPTH, DEPTH), DEPTH)
        tt[...] = jnp.dot(l_ref[comps, :], u_ref[row], preferred_element_type=F32)
        table[...] = tab_ref[block]

    def strips(f):
        for j in range(DEPTH // STRIP):
            rows = slice(j * STRIP, (j + 1) * STRIP)

            def put(i, v, rows=rows):
                f[i, rows] = v

            yield from factors(tt[rows], put)

    def product(d, f, table):
        pair, which = d // 4, d % 4
        a, k = pair // 4, pair % 4
        x = 6 * a + (3 if which in (1, 2) else 0)
        y = 12 + 4 * k + (2 if which in (1, 3) else 0)
        t = table[pair]
        hi = f[x] * f[y]
        both = jnp.dot(t, hi, preferred_element_type=F32)
        yield
        lo = f[x + 1] * f[y] + f[x + 2] * f[y + 1]
        both += jnp.dot(t, lo, preferred_element_type=F32)
        yield
        acc[pair, which] += both

    def step(f, g, table):
        ahead, done, count = strips(g), 0, 0
        for d in range(32):
            for _ in product(d, f, table):
                count += 1
                while done < count * PIECES * (DEPTH // STRIP) // 64:
                    next(ahead, None)
                    done += 1
        for _ in ahead:
            pass

    def flush(row):
        sign = jnp.where(lax.broadcasted_iota(jnp.int32, (8, LANES), 0) < 4, -1.0, 1.0)
        for pair in range(8):
            a, k = pair // 4, pair % 4
            p = [(acc[pair, w, 0:8] + acc[pair, w, 8:16]) * (1.0 / 256.0) for w in range(4)]
            c = p[0] + sign * p[1]
            s = p[2] - sign * p[3]
            plus, minus = (2 * a + 1) ^ info_ref[0], (2 * a) ^ info_ref[0]
            o_ref[plus & 1, plus >> 1, row, k] = jnp.concatenate([c[0:4], s[0:4]], axis=0)
            o_ref[minus & 1, minus >> 1, row, 3 - k] = jnp.concatenate([c[4:8], s[4:8]], axis=0)
        acc[...] = jnp.zeros_like(acc)

    o_ref[...] = jnp.zeros_like(o_ref)
    acc[...] = jnp.zeros_like(acc)
    begin(0, ta)
    for _ in strips(fa):
        pass

    def body(i, carry):
        begin(2 * i + 1, tb)
        step(fa, fb, ta)
        begin(2 * i + 2, ta)
        step(fb, fa, tb)

        @pl.when(lax.rem(2 * i + 2, blocks) == 0)
        def _():
            flush(lax.div(2 * i, blocks))

        return carry

    lax.fori_loop(0, total // 2, body, 0)


def predict(info, heads, position, flux):
    comps = position.shape[1]
    row_blocks, blocks = GROUP, comps // DEPTH
    l_coord, m_coord = position[0], position[1]
    n_minus = jnp.sqrt(1.0 - l_coord * l_coord - m_coord * m_coord) - 1.0
    lp = pieces(jnp.pad(jnp.stack([l_coord, m_coord, n_minus]), ((0, 5), (0, 0))), 3)
    l = jnp.concatenate([lp[j] for _, j in TERMS]).T
    i, q, v, w = flux
    bright = jnp.stack([i + q, v, w, i - q], 1).reshape(2, 8, 4, comps)
    plus, minus = bright[:, 4:].reshape(8, 4, comps), bright[:, 3::-1].reshape(8, 4, comps)
    hi, lo = pieces(jnp.concatenate([plus, minus], 1), 2)
    table = jnp.concatenate([hi, lo], 1).reshape(8, 16, blocks, DEPTH).transpose(2, 0, 1, 3)
    vmem = pl.BlockSpec(memory_space=pltpu.VMEM)
    return pl.pallas_call(
        lambda *refs: predict_kernel(blocks, *refs),
        out_shape=jax.ShapeDtypeStruct((2, 2, row_blocks, 4, 8, LANES), F32),
        in_specs=[pl.BlockSpec(memory_space=pltpu.SMEM)] + [vmem] * 6,
        out_specs=vmem,
        scratch_shapes=[
            pltpu.VMEM((FACTORS, DEPTH, LANES), BF16),
            pltpu.VMEM((FACTORS, DEPTH, LANES), BF16),
            pltpu.VMEM((DEPTH, LANES), F32),
            pltpu.VMEM((8, 16, DEPTH), BF16),
            pltpu.VMEM((8, 16, DEPTH), BF16),
            pltpu.VMEM((8, 4, 16, LANES), F32),
            pltpu.VMEM((row_blocks + 1, 8, LANES), F32),
            pltpu.VMEM((row_blocks, 48, LANES), BF16),
        ],
        compiler_params=pltpu.CompilerParams(vmem_limit_bytes=40 << 20),
        cost_estimate=pl.CostEstimate(
            flops=64 * 16 * GROUP * LANES * comps, bytes_accessed=4 << 20, transcendentals=0
        ),
        name="predict",
    )(info, *heads, l, table)


def prepare_kernel(info_ref, h0, h1, h2, h3, table_ref, obs_ref, slot_ref, picked_ref, gain_ref):
    slots = table_ref.shape[1]
    flip = info_ref[1]
    starts, counts, live = group_rows(info_ref, (h0, h1, h2, h3))
    obs_ref[...] = jnp.zeros_like(obs_ref)
    slot_ref[...] = jnp.zeros_like(slot_ref)
    for b, head in enumerate((h0, h1, h2, h3)):
        place(slot_ref, head[0:8], starts[b], counts[b])
        place(obs_ref, head[8:40], starts[b], counts[b])
    rest = table_ref[...]
    for p in range(3):
        part = rest.astype(BF16)
        gain_ref[64 * p : 64 * p + 64] = part
        rest = rest - part.astype(F32)

    def block(row, carry):
        lane = lax.broadcasted_iota(jnp.int32, (1, LANES), 1)
        time = [(lax.rem(lane, TIMES) == t).astype(F32) for t in range(TIMES)]
        slot = lax.broadcasted_iota(jnp.int32, (slots, LANES), 0)
        for end in range(2):
            at = slot_ref[row, 3 + end : 4 + end].astype(jnp.int32)
            hot = jnp.where(slot == (at ^ flip), 1.0, 0.0).astype(BF16)
            g = jnp.dot(gain_ref[...], hot, preferred_element_type=F32)
            g = g[0:64] + g[64:128] + g[128:192]
            picked_ref[row, end] = sum(g[16 * t : 16 * t + 16] * time[t] for t in range(TIMES))
        return carry

    lax.fori_loop(0, lax.div(live + LANES - 1, LANES), block, 0)


def calibrate_kernel(info_ref, h0, h1, h2, h3, obs_ref, slot_ref, picked_ref, own_ref, near_ref, far_ref, out_ref, sum_ref, res_ref, norm_ref):
    slots = norm_ref.shape[0]
    starts, counts, live = group_rows(info_ref, (h0, h1, h2, h3))
    norm_ref[...] = jnp.zeros_like(norm_ref)
    res_ref[...] = jnp.zeros_like(res_ref)

    def block(row, carry):
        lane = lax.broadcasted_iota(jnp.int32, (1, LANES), 1)
        weight = (lane + row * LANES < live).astype(F32)
        time = [(lax.rem(lane, TIMES) == t).astype(F32) for t in range(TIMES)]
        slot = lax.broadcasted_iota(jnp.int32, (slots, LANES), 0)
        hots, gains = [], []
        for end in range(2):
            at = slot_ref[row, 3 + end : 4 + end].astype(jnp.int32)
            hots.append(jnp.where(slot == at, 1.0, 0.0).astype(BF16))
            picked = picked_ref[row, end]
            gains.append([[picked[8 * part + 4 * pol : 8 * part + 4 * pol + 4] for pol in range(2)] for part in range(2)])
        sums = own_ref[row] + near_ref[row] + far_ref[row]
        c = [sums[:, n] for n in range(4)]
        s = [sums[:, 4 + n] for n in range(4)]
        vis_r = [[c[0], c[1] + s[2]], [c[1] - s[2], c[3]]]
        vis_i = [[-s[0], c[2] - s[1]], [-c[2] - s[1], -s[3]]]
        (near_r, near_i), (far_r, far_i) = gains
        near = [[0.0, 0.0], [0.0, 0.0], [0.0, 0.0]]
        far = [[0.0, 0.0], [0.0, 0.0], [0.0, 0.0]]
        for a in range(2):
            for b in range(2):
                vr, vi = vis_r[a][b], vis_i[a][b]
                zr = far_r[b] * vr + far_i[b] * vi
                zi = far_r[b] * vi - far_i[b] * vr
                yr = near_r[a] * vr - near_i[a] * vi
                yi = near_r[a] * vi + near_i[a] * vr
                mr = near_r[a] * zr - near_i[a] * zi
                mi = near_r[a] * zi + near_i[a] * zr
                at = (a * 2 + b) * 4
                rr = weight * (obs_ref[row, at : at + 4] - mr)
                ri = weight * (obs_ref[row, 16 + at : 16 + at + 4] - mi)
                res_ref[row, at : at + 4] = rr
                res_ref[row, 16 + at : 16 + at + 4] = ri
                near[0][a] += weight * (zr * zr + zi * zi)
                near[1][a] += zr * rr + zi * ri
                near[2][a] += zr * ri - zi * rr
                far[0][b] += weight * (yr * yr + yi * yi)
                far[1][b] += yr * rr + yi * ri
                far[2][b] += yi * rr - yr * ri
        terms = []
        for end in (near, far):
            flat = jnp.concatenate([end[k][pol] for k in range(3) for pol in range(2)], axis=0)
            whole = jnp.concatenate([flat * time[t] for t in range(TIMES)], axis=0)
            hi = whole.astype(BF16)
            lo = (whole - hi.astype(F32)).astype(BF16)
            terms.append(jnp.concatenate([hi, lo], axis=0))
        both = lax.dot_general(
            jnp.concatenate(hots, axis=1),
            jnp.concatenate(terms, axis=1),
            (((1,), (1,)), ((), ())),
            preferred_element_type=F32,
        )
        norm_ref[...] += both
        return carry

    lax.fori_loop(0, lax.div(live + LANES - 1, LANES), block, 0)
    sum_ref[...] = norm_ref[:, :96] + norm_ref[:, 96:]
    for b in range(GROUP):
        out_ref[b] = taken(res_ref, starts[b], counts[b])


VMEM = pl.BlockSpec(memory_space=pltpu.VMEM)
SMEM = pl.BlockSpec(memory_space=pltpu.SMEM)


def prepare(info, heads, table):
    return pl.pallas_call(
        prepare_kernel,
        out_shape=(
            jax.ShapeDtypeStruct((GROUP + 1, 32, LANES), F32),
            jax.ShapeDtypeStruct((GROUP + 1, 8, LANES), F32),
            jax.ShapeDtypeStruct((GROUP, 2, 16, LANES), F32),
        ),
        in_specs=[SMEM] + [VMEM] * 5,
        out_specs=(VMEM, VMEM, VMEM),
        scratch_shapes=[pltpu.VMEM((192, table.shape[1]), BF16)],
        compiler_params=pltpu.CompilerParams(vmem_limit_bytes=16 << 20),
        cost_estimate=pl.CostEstimate(flops=1 << 30, bytes_accessed=1 << 20, transcendentals=0),
        name="prepare",
    )(info, *heads, table)


def calibrate(info, heads, ready, parts, antennas):
    return pl.pallas_call(
        calibrate_kernel,
        out_shape=(
            jax.ShapeDtypeStruct((GROUP, 32, LANES), F32),
            jax.ShapeDtypeStruct((antennas, 96), F32),
        ),
        in_specs=[SMEM] + [VMEM] * 10,
        out_specs=(VMEM, VMEM),
        scratch_shapes=[
            pltpu.VMEM((GROUP + 1, 32, LANES), F32),
            pltpu.VMEM((antennas, 192), F32),
        ],
        compiler_params=pltpu.CompilerParams(vmem_limit_bytes=24 << 20),
        name="calibrate",
    )(info, *heads, *ready, *parts)


def swap(value, axis, bits):
    count = lax.axis_size(axis)
    return lax.ppermute(value, axis, [(d, d ^ bits) for d in range(count)])


def relative(values, core, chip):
    values = [jnp.where(core, values[j ^ 1], values[j]) for j in range(GROUP)]
    return [jnp.where(chip, values[j ^ 2], values[j]) for j in range(GROUP)]


def exchange(values):
    return [values[0]] + [swap(values[b], "comp", b) for b in range(1, GROUP)]


def owner_slots(antenna_owner, per_owner):
    index = jnp.arange(antenna_owner.shape[0], dtype=jnp.int32)
    same = (antenna_owner[None, :] == antenna_owner[:, None]) & (index[None, :] < index[:, None])
    return antenna_owner * per_owner + jnp.sum(same.astype(jnp.int32), axis=1)


def row_slots(antennas, slots):
    index = jnp.arange(slots.shape[0], dtype=jnp.int32)
    return jnp.sum(jnp.where(antennas[..., None] == index, slots, 0), axis=-1)


def local(baseline_uvw, antenna_pair, row_count, comp_position, comp_flux, gain, antenna_owner, observed):
    rows = baseline_uvw.shape[1]
    antennas = antenna_owner.shape[0]
    lines = lax.axis_size("bl")
    per_owner = antennas // (lines * GROUP)
    me_comp, me_line = lax.axis_index("comp"), lax.axis_index("bl")
    core, chip = (me_comp & 1) != 0, me_comp >= 2

    slots = row_slots(antenna_pair, owner_slots(antenna_owner, per_owner))
    count = jnp.broadcast_to(row_count[:, None], (3, rows))
    head = jnp.concatenate([baseline_uvw, slots.astype(F32), count.astype(F32)])
    part = gain.reshape(per_owner, 16, GROUP, 4).transpose(2, 1, 3, 0).reshape(GROUP, -1, rows)
    part = relative(list(part), core, chip)
    obs = observed.reshape(rows, 8, GROUP, 4).transpose(2, 1, 3, 0).reshape(GROUP, 32, rows)
    obs = relative(list(obs), core, chip)
    heads = exchange([jnp.concatenate([head, o, p]) for o, p in zip(obs, part)])
    info = jnp.stack([me_comp, (me_line * GROUP + me_comp) * per_owner]).astype(jnp.int32)

    mine = jnp.concatenate([h[40:] for h in heads])
    even = jnp.stack([mine] + [swap(mine, "bl", b) for b in range(2, lines, 2)])

    sums = predict(info, heads, comp_position, comp_flux)

    first = swap(sums[1], "comp", 1)
    odd = swap(even, "bl", 1)
    half = sums[0, 1] + first[1]
    second = swap(half, "comp", 2)
    odd, _ = lax.optimization_barrier((odd, half))
    table = jnp.stack([even, odd], 1).reshape(lines, GROUP, 64, per_owner)
    table = table.transpose(2, 0, 1, 3).reshape(64, antennas)

    ready = prepare(info, heads, table)
    res, norm = calibrate(info, heads, ready, (sums[0, 0], first[0], second), antennas)

    res = exchange(list(res))
    norm = lax.all_to_all(norm.reshape(lines * GROUP, per_owner, 96), ("bl", "comp"), 0, 0)
    norm = jnp.sum(norm.reshape(lines, GROUP, per_owner, 24, 4), axis=0)
    normal = norm.transpose(1, 2, 0, 3).reshape(per_owner, 24 * CHANNELS)
    res = jnp.stack(relative(res, core, chip))
    residual = res.reshape(GROUP, 8, 4, rows).transpose(3, 1, 0, 2).reshape(rows, 8 * CHANNELS)
    return (residual, normal)


def solution(mesh):
    rows = P(("bl", "comp"))
    return jax.shard_map(
        local,
        mesh=mesh,
        in_specs=(
            P(None, ("bl", "comp")),
            P(None, ("bl", "comp")),
            rows,
            P(None, "comp"),
            P(None, None, "comp"),
            P(("bl", "comp"), None),
            P(),
            P(("bl", "comp"), None),
        ),
        out_specs=(P(("bl", "comp"), None), P(("bl", "comp"), None)),
        check_vma=False,
    )
```

profile of v0, /device:TPU:0, one launch (start us, length us, event | category | flops | bytes accessed | tf_op | source)
XLA Modules:
  0.0 116.4 jit_solution(14689327613473477316)
XLA Ops:
  1.3 0.2 convert_reduce_fusion
  1.6 0.3 select_reduce_fusion
  2.1 0.8 copy-done.2
  3.1 0.6 copy-done.3
  3.8 3.0 %collective-permute-start.1 = (f32[44,256]{1,0:T(8,128)S(1)}, f32[44,256]{1,0:T(8,128)S(1)}, u32[]{:S(2)}, u32[]{:S(2)}) collective-permute-start(f32[44,256]{1,0:T(8,128)S(1)} %concatenate.40), channel_id=1, source_target_pairs={{0,2},{1,3},{2,0},{3,1},{4,6},{5,7},{6,4},{7,5},{8,10},{9,11},{10,... | collective-permute-start | bytes 135176 | tf_op jit(solution)/shard_map/ppermute | solution.py:356
  7.1 0.2 collective-permute-start.2
  7.3 0.5 copy-done
  8.2 0.1 copy.63
  8.7 0.5 pad_maximum_fusion
  9.7 0.1 reduce-precision_convert_fusion
  10.1 0.3 copy.59
  10.5 0.2 collective-permute-done.2.refs_4_.h3
  10.7 2.7 %collective-permute-start.4 = (f32[16,256]{1,0:T(8,128)S(1)}, f32[16,256]{1,0:T(8,128)S(1)}, u32[]{:S(2)}, u32[]{:S(2)}) collective-permute-start(f32[16,256]{1,0:T(8,128)S(1)} %get-tuple-element.46), channel_id=1, source_target_pairs={{0,16},{4,20},{8,24},{12,28},{16,0},{20,4},{24,8},{28,12},{1,17},{... | collective-permute-start | bytes 49160 | tf_op jit(solution)/shard_map/ppermute | solution.py:356
  13.4 1.6 %collective-permute-start.3 = (f32[16,256]{1,0:T(8,128)S(1)}, f32[16,256]{1,0:T(8,128)S(1)}, u32[]{:S(2)}, u32[]{:S(2)}) collective-permute-start(f32[16,256]{1,0:T(8,128)S(1)} %get-tuple-element.46), channel_id=1, source_target_pairs={{0,8},{4,12},{8,0},{12,4},{16,24},{20,28},{24,16},{28,20},{1,9},{5... | collective-permute-start | bytes 49160 | tf_op jit(solution)/shard_map/ppermute | solution.py:356
  14.9 0.2 collective-permute-start.5
  15.2 38.1 %predict.1 = f32[2,2,4,4,8,256]{5,4,3,2,1,0:T(8,128)S(1)} custom-call(s32[2]{0:T(128)S(1)} %pad_add_fusion.refs_0_.info_ref, f32[44,256]{1,0:T(8,128)S(1)} %concatenate.38.refs_1_.h0, f32[44,256]{1,0:T(8,128)S(1)} %collective-permute-done.refs_2_.h1, f32[44,256]{1,0:T(8,128)S(1)} %collective-permute-done.1.refs_3_.h2, ...), custom_call_target="tpu_custom_call" | custom-call | flops 2147483648 | bytes 4194304 | tf_op jit(solution)/shard_map/predict/pallas_call | solution.py:195
  53.4 37.8 %collective-permute-start.6 = (f32[4,16,256]{2,1,0:T(8,128)S(1)}, f32[4,16,256]{2,1,0:T(8,128)S(1)}, u32[]{:S(2)}, u32[]{:S(2)}) collective-permute-start(f32[4,16,256]{2,1,0:T(8,128)S(1)} %get-tuple-element.44), channel_id=1, source_target_pairs={{0,4},{4,0},{8,12},{12,8},{16,20},{20,16},{24,28},{28,24},{1,5},{5... | collective-permute-start | bytes 196616 | tf_op jit(solution)/shard_map/ppermute | solution.py:356
  91.2 1.4 %collective-permute-start.8 = (f32[4,4,8,256]{3,2,1,0:T(8,128)S(1)}, f32[4,4,8,256]{3,2,1,0:T(8,128)S(1)}, u32[]{:S(2)}, u32[]{:S(2)}) collective-permute-start(f32[4,4,8,256]{3,2,1,0:T(8,128)S(1)} %fusion.3), channel_id=1, source_target_pairs={{0,2},{1,3},{2,0},{3,1},{4,6},{5,7},{6,4},{7,5},{8,10},{9,11},{10,... | collective-permute-start | bytes 393224 | tf_op jit(solution)/shard_map/ppermute | solution.py:356
  92.6 1.3 %collective-permute-done.6 = f32[4,16,256]{2,1,0:T(8,128)S(1)} collective-permute-done((f32[4,16,256]{2,1,0:T(8,128)S(1)}, f32[4,16,256]{2,1,0:T(8,128)S(1)}, u32[]{:S(2)}, u32[]{:S(2)}) %collective-permute-start.6) | collective-permute-done | bytes 65568 | tf_op jit(solution)/shard_map/ppermute | solution.py:356
  94.0 0.3 reshape.154
  94.3 0.3 copy.67
  94.8 1.4 %prepare.1 = (f32[5,32,256]{2,1,0:T(8,128)S(1)}, f32[5,8,256]{2,1,0:T(8,128)S(1)}, f32[4,2,16,256]{3,2,1,0:T(8,128)S(1)}) custom-call(s32[2]{0:T(128)S(1)} %pad_add_fusion.refs_0_.info_ref, f32[44,256]{1,0:T(8,128)S(1)} %concatenate.38.refs_1_.h0, f32[44,256]{1,0:T(8,128)S(1)} %collective-permute-done.refs_2_.h1, ...), custom_call_target="tpu_custom_call" | custom-call | flops 1073741824 | bytes 1048576 | tf_op jit(solution)/shard_map/prepare/pallas_call | solution.py:320
  96.1 0.8 collective-permute-done.8.far_ref
  96.9 2.4 %calibrate.1 = (f32[4,32,256]{2,1,0:T(8,128)S(1)}, f32[512,96]{1,0:T(8,128)}) custom-call(s32[2]{0:T(128)S(1)} %pad_add_fusion.refs_0_.info_ref, f32[44,256]{1,0:T(8,128)S(1)} %concatenate.38.refs_1_.h0, f32[44,256]{1,0:T(8,128)S(1)} %collective-permute-done.refs_2_.h1, f32[44,256]{1,0:T(8,128)S(1)} %collective-permute-done.1.refs_3_.h2, ...), custom_call_target="tpu_custom_call" | custom-call | tf_op jit(solution)/shard_map/calibrate/pallas_call | solution.py:337
  99.3 5.6 %all-to-all-start = ((f32[32,16,96]{2,1,0:T(8,128)}), f32[32,16,96]{2,1,0:T(8,128)S(1)}, u32[]{:S(2)}, u32[]{:S(2)}) async-start(f32[32,16,96]{2,1,0:T(8,128)} %bitcast.35), calls=%async_computation | async-start | bytes 524288 | tf_op jit(solution)/shard_map/all_to_all | solution.py:414
  104.9 0.3 collective-permute-start.11
  105.2 1.7 %collective-permute-start.10 = (f32[32,256]{1,0:T(8,128)S(1)}, f32[32,256]{1,0:T(8,128)S(1)}, u32[]{:S(2)}, u32[]{:S(2)}) collective-permute-start(f32[32,256]{1,0:T(8,128)S(1)} %get-tuple-element.33), channel_id=1, source_target_pairs={{0,2},{1,3},{2,0},{3,1},{4,6},{5,7},{6,4},{7,5},{8,10},{9,11},{10,... | collective-permute-start | bytes 98312 | tf_op jit(solution)/shard_map/ppermute | solution.py:356
  106.9 2.5 %collective-permute-done.10 = f32[32,256]{1,0:T(8,128)S(1)} collective-permute-done((f32[32,256]{1,0:T(8,128)S(1)}, f32[32,256]{1,0:T(8,128)S(1)}, u32[]{:S(2)}, u32[]{:S(2)}) %collective-permute-start.10) | collective-permute-done | bytes 32800 | tf_op jit(solution)/shard_map/ppermute | solution.py:356
  109.4 1.5 %collective-permute-done.9 = f32[32,256]{1,0:T(8,128)S(1)} collective-permute-done((f32[32,256]{1,0:T(8,128)S(1)}, f32[32,256]{1,0:T(8,128)S(1)}, u32[]{:S(2)}, u32[]{:S(2)}) %collective-permute-start.9) | collective-permute-done | bytes 32800 | tf_op jit(solution)/shard_map/ppermute | solution.py:356
  111.1 0.8 copy.75
  111.9 3.6 %all-to-all-done = f32[32,16,96]{2,1,0:T(8,128)S(1)} async-done(((f32[32,16,96]{2,1,0:T(8,128)}), f32[32,16,96]{2,1,0:T(8,128)S(1)}, u32[]{:S(2)}, u32[]{:S(2)}) %all-to-all-start) | async-done | bytes 196640 | tf_op jit(solution)/shard_map/all_to_all | solution.py:414
  115.7 0.7 copy.76
  (83 shorter events, 2.9 us)
Async XLA Ops:
  0.6 1.0 copy-start.6
  0.6 0.7 copy-start.4
  0.7 1.2 %copy-start.5 = (f32[16,256]{1,0:T(8,128)S(1)}, f32[16,256]{1,0:T(8,128)}, u32[]{:S(2)}) copy-start(f32[16,256]{1,0:T(8,128)} %param.13) | copy-start | bytes 49156
  2.0 0.9 copy-start.2
  3.0 0.7 copy-start.3
  3.1 5.0 %copy-start.1 = (f32[4,16,2048]{2,1,0:T(8,128)S(1)}, f32[4,16,2048]{2,1,0:T(8,128)}, u32[]{:S(2)}) copy-start(f32[4,16,2048]{2,1,0:T(8,128)} %param.12) | copy-start | bytes 1572868
  3.8 6.7 %collective-permute-start.1 = (f32[44,256]{1,0:T(8,128)S(1)}, f32[44,256]{1,0:T(8,128)S(1)}, u32[]{:S(2)}, u32[]{:S(2)}) collective-permute-start(f32[44,256]{1,0:T(8,128)S(1)} %concatenate.40), channel_id=1, source_target_pairs={{0,2},{1,3},{2,0},{3,1},{4,6},{5,7},{6,4},{7,5},{8,10},{9,11},{10,... | collective-permute-start | bytes 135176 | tf_op jit(solution)/shard_map/ppermute | solution.py:356
  6.9 3.6 %collective-permute-start = (f32[44,256]{1,0:T(8,128)S(1)}, f32[44,256]{1,0:T(8,128)S(1)}, u32[]{:S(2)}, u32[]{:S(2)}) collective-permute-start(f32[44,256]{1,0:T(8,128)S(1)} %concatenate.39), channel_id=1, source_target_pairs={{0,1},{1,0},{2,3},{3,2},{4,5},{5,4},{6,7},{7,6},{8,9},{9,8},{10,11... | collective-permute-start | bytes 135176 | tf_op jit(solution)/shard_map/ppermute | solution.py:356
  7.1 0.7 copy-start
  7.1 3.6 %collective-permute-start.2 = (f32[44,256]{1,0:T(8,128)S(1)}, f32[44,256]{1,0:T(8,128)S(1)}, u32[]{:S(2)}, u32[]{:S(2)}) collective-permute-start(f32[44,256]{1,0:T(8,128)S(1)} %concatenate.41), channel_id=1, source_target_pairs={{0,3},{1,2},{2,1},{3,0},{4,7},{5,6},{6,5},{7,4},{8,11},{9,10},{10,... | collective-permute-start | bytes 135176 | tf_op jit(solution)/shard_map/ppermute | solution.py:356
  10.7 42.7 %collective-permute-start.4 = (f32[16,256]{1,0:T(8,128)S(1)}, f32[16,256]{1,0:T(8,128)S(1)}, u32[]{:S(2)}, u32[]{:S(2)}) collective-permute-start(f32[16,256]{1,0:T(8,128)S(1)} %get-tuple-element.46), channel_id=1, source_target_pairs={{0,16},{4,20},{8,24},{12,28},{16,0},{20,4},{24,8},{28,12},{1,17},{... | collective-permute-start | bytes 49160 | tf_op jit(solution)/shard_map/ppermute | solution.py:356
  13.4 40.0 %collective-permute-start.3 = (f32[16,256]{1,0:T(8,128)S(1)}, f32[16,256]{1,0:T(8,128)S(1)}, u32[]{:S(2)}, u32[]{:S(2)}) collective-permute-start(f32[16,256]{1,0:T(8,128)S(1)} %get-tuple-element.46), channel_id=1, source_target_pairs={{0,8},{4,12},{8,0},{12,4},{16,24},{20,28},{24,16},{28,20},{1,9},{5... | collective-permute-start | bytes 49160 | tf_op jit(solution)/shard_map/ppermute | solution.py:356
  14.9 38.4 %collective-permute-start.5 = (f32[16,256]{1,0:T(8,128)S(1)}, f32[16,256]{1,0:T(8,128)S(1)}, u32[]{:S(2)}, u32[]{:S(2)}) collective-permute-start(f32[16,256]{1,0:T(8,128)S(1)} %get-tuple-element.46), channel_id=1, source_target_pairs={{0,24},{4,28},{8,16},{12,20},{16,8},{20,12},{24,0},{28,4},{1,25},{... | collective-permute-start | bytes 49160 | tf_op jit(solution)/shard_map/ppermute | solution.py:356
  53.3 37.9 %collective-permute-start.7 = (f32[2,4,4,8,256]{4,3,2,1,0:T(8,128)S(1)}, f32[2,4,4,8,256]{4,3,2,1,0:T(8,128)S(1)}, u32[]{:S(2)}, u32[]{:S(2)}) collective-permute-start(f32[2,4,4,8,256]{4,3,2,1,0:T(8,128)S(1)} %slice_bitcast_fusion), channel_id=1, source_target_pairs={{0,1},{1,0},{2,3},{3,2},{4,5},{5,4},{6,7},{7,6},{8,9},{9,8},{10,11... | collective-permute-start | bytes 786440 | tf_op jit(solution)/shard_map/ppermute | solution.py:356
  53.4 40.5 %collective-permute-start.6 = (f32[4,16,256]{2,1,0:T(8,128)S(1)}, f32[4,16,256]{2,1,0:T(8,128)S(1)}, u32[]{:S(2)}, u32[]{:S(2)}) collective-permute-start(f32[4,16,256]{2,1,0:T(8,128)S(1)} %get-tuple-element.44), channel_id=1, source_target_pairs={{0,4},{4,0},{8,12},{12,8},{16,20},{20,16},{24,28},{28,24},{1,5},{5... | collective-permute-start | bytes 196616 | tf_op jit(solution)/shard_map/ppermute | solution.py:356
  91.2 5.7 %collective-permute-start.8 = (f32[4,4,8,256]{3,2,1,0:T(8,128)S(1)}, f32[4,4,8,256]{3,2,1,0:T(8,128)S(1)}, u32[]{:S(2)}, u32[]{:S(2)}) collective-permute-start(f32[4,4,8,256]{3,2,1,0:T(8,128)S(1)} %fusion.3), channel_id=1, source_target_pairs={{0,2},{1,3},{2,0},{3,1},{4,6},{5,7},{6,4},{7,5},{8,10},{9,11},{10,... | collective-permute-start | bytes 393224 | tf_op jit(solution)/shard_map/ppermute | solution.py:356
  99.3 16.2 %all-to-all-start = ((f32[32,16,96]{2,1,0:T(8,128)}), f32[32,16,96]{2,1,0:T(8,128)S(1)}, u32[]{:S(2)}, u32[]{:S(2)}) async-start(f32[32,16,96]{2,1,0:T(8,128)} %bitcast.35), calls=%async_computation | async-start | bytes 524288 | tf_op jit(solution)/shard_map/all_to_all | solution.py:414
  104.9 2.0 %collective-permute-start.11 = (f32[32,256]{1,0:T(8,128)S(1)}, f32[32,256]{1,0:T(8,128)S(1)}, u32[]{:S(2)}, u32[]{:S(2)}) collective-permute-start(f32[32,256]{1,0:T(8,128)S(1)} %get-tuple-element.32), channel_id=1, source_target_pairs={{0,1},{1,0},{2,3},{3,2},{4,5},{5,4},{6,7},{7,6},{8,9},{9,8},{10,11... | collective-permute-start | bytes 98312 | tf_op jit(solution)/shard_map/ppermute | solution.py:356
  105.2 4.2 %collective-permute-start.10 = (f32[32,256]{1,0:T(8,128)S(1)}, f32[32,256]{1,0:T(8,128)S(1)}, u32[]{:S(2)}, u32[]{:S(2)}) collective-permute-start(f32[32,256]{1,0:T(8,128)S(1)} %get-tuple-element.33), channel_id=1, source_target_pairs={{0,2},{1,3},{2,0},{3,1},{4,6},{5,7},{6,4},{7,5},{8,10},{9,11},{10,... | collective-permute-start | bytes 98312 | tf_op jit(solution)/shard_map/ppermute | solution.py:356
  106.9 4.1 %collective-permute-start.9 = (f32[32,256]{1,0:T(8,128)S(1)}, f32[32,256]{1,0:T(8,128)S(1)}, u32[]{:S(2)}, u32[]{:S(2)}) collective-permute-start(f32[32,256]{1,0:T(8,128)S(1)} %get-tuple-element.34), channel_id=1, source_target_pairs={{0,3},{1,2},{2,1},{3,0},{4,7},{5,6},{6,5},{7,4},{8,11},{9,10},{10,... | collective-permute-start | bytes 98312 | tf_op jit(solution)/shard_map/ppermute | solution.py:356
where the time goes:
time: 117 us; the launch traced here: 116 us
  starting transfers between devices  54.5 us (47%)
  Pallas kernels  41.8 us (36%)
  waiting for transfers between devices  9.96 us (9%)
  local copies, waits for them, and re-layouts  6.62 us (6%)
  between operations  1.82 us (2%)
  other arithmetic  1.68 us (1%)
    ppermute x12, starting transfers between devices, swap(): return lax.ppermute(value, axis, [(d, d ^ bits) for d in range(count)])  48.9 us
    pallas_call x1, Pallas kernels, predict(): pl.pallas_call(lambda *refs: predict_kernel(blocks, *refs), out_shape=jax...  38.1 us
    ppermute x12, waiting for transfers between devices, swap(): return lax.ppermute(value, axis, [(d, d ^ bits) for d in range(count)])  6.38 us
    all_to_all x1, starting transfers between devices, local(): lax.all_to_all(norm.reshape(lines * GROUP, per_owner, 96), ('bl', 'comp')...  5.58 us
    unnamed x19, local copies, waits for them, and re-layouts  3.68 us
    all_to_all x1, waiting for transfers between devices, local(): lax.all_to_all(norm.reshape(lines * GROUP, per_owner, 96), ('bl', 'comp')...  3.57 us
    pallas_call x1, Pallas kernels, calibrate(): pl.pallas_call(calibrate_kernel, out_shape=(jax.ShapeDtypeStruct((GROUP,...  2.4 us
  transfers between devices with their start and end apart: 13, of which 6 were waited for; matrix products, arithmetic and copies ran while one was open for 4% of the time, Pallas kernels for 34%

commit v1 on v0

--- a/solution.py
+++ b/solution.py
@@ -91,9 +91,14 @@
     return jnp.where(lane < count, jnp.where(lane < LANES - off, first, second), 0.0)
 
 
-def predict_kernel(blocks, info_ref, h0, h1, h2, h3, l_ref, tab_ref, o_ref, fa, fb, tt, ta, tb, acc, rows_ref, u_ref):
+def predict_kernel(blocks, info_ref, h0, h1, h2, h3, l_ref, tab_ref, o_ref, fa, fb, tt, ta, tb, acc, acc2, rows_ref, u_ref):
     starts, counts, live = group_rows(info_ref, (h0, h1, h2, h3))
-    total = lax.div(live + LANES - 1, LANES) * blocks
+    half = LANES // 2
+    rest_rows = lax.rem(live, LANES)
+    halved = (rest_rows > 0) & (rest_rows <= half)
+    full = lax.div(live + half - 1, LANES)
+    total = full * blocks
+    last = total + jnp.where(halved, blocks // 2, 0) - 1
     rows_ref[...] = jnp.zeros_like(rows_ref)
     for b, head in enumerate((h0, h1, h2, h3)):
         place(rows_ref, head[0:8], starts[b], counts[b])
@@ -103,14 +108,22 @@
             part = rest.astype(BF16).astype(F32)
             parts.append(part)
             rest = rest - part
-        u_ref[row] = jnp.concatenate([parts[i] for i, _ in TERMS], axis=0).astype(BF16)
+        u = jnp.concatenate([parts[i] for i, _ in TERMS], axis=0).astype(BF16)
+        u_ref[row, 0] = u[:, :half]
+        u_ref[row, 1] = u[:, half:]
 
     def begin(index, table):
-        index = jnp.minimum(index, total - 1)
-        row, block = lax.div(index, blocks), lax.rem(index, blocks)
-        comps = pl.ds(pl.multiple_of(block * DEPTH, DEPTH), DEPTH)
-        tt[...] = jnp.dot(l_ref[comps, :], u_ref[row], preferred_element_type=F32)
-        table[...] = tab_ref[block]
+        index = jnp.minimum(index, last)
+        extra = index - total
+        pair = extra >= 0
+        row = jnp.where(pair, full, lax.div(index, blocks))
+        left = jnp.where(pair, 2 * extra, lax.rem(index, blocks))
+        right = jnp.where(pair, left + 1, left)
+        for side, block in enumerate((left, right)):
+            comps = pl.ds(pl.multiple_of(block * DEPTH, DEPTH), DEPTH)
+            u = u_ref[row, jnp.where(pair, 0, side)]
+            tt[:, side * half : side * half + half] = jnp.dot(l_ref[comps, :], u, preferred_element_type=F32)
+            table[:, 16 * side : 16 * side + 16] = tab_ref[block]
 
     def strips(f):
         for j in range(DEPTH // STRIP):
@@ -121,24 +134,24 @@
 
             yield from factors(tt[rows], put)
 
-    def product(d, f, table):
+    def product(d, f, table, into):
         pair, which = d // 4, d % 4
         a, k = pair // 4, pair % 4
         x = 6 * a + (3 if which in (1, 2) else 0)
         y = 12 + 4 * k + (2 if which in (1, 3) else 0)
-        t = table[pair]
+        t = table[pair, 0 : into.shape[2]]
         hi = f[x] * f[y]
         both = jnp.dot(t, hi, preferred_element_type=F32)
         yield
         lo = f[x + 1] * f[y] + f[x + 2] * f[y + 1]
         both += jnp.dot(t, lo, preferred_element_type=F32)
         yield
-        acc[pair, which] += both
-
-    def step(f, g, table):
+        into[pair, which] += both
+
+    def step(f, g, table, into):
         ahead, done, count = strips(g), 0, 0
         for d in range(32):
-            for _ in product(d, f, table):
+            for _ in product(d, f, table, into):
                 count += 1
                 while done < count * PIECES * (DEPTH // STRIP) // 64:
                     next(ahead, None)
@@ -164,11 +177,14 @@
     for _ in strips(fa):
         pass
 
+    def twice(first, into):
+        begin(first + 1, tb)
+        step(fa, fb, ta, into)
+        begin(first + 2, ta)
+        step(fb, fa, tb, into)
+
     def body(i, carry):
-        begin(2 * i + 1, tb)
-        step(fa, fb, ta)
-        begin(2 * i + 2, ta)
-        step(fb, fa, tb)
+        twice(2 * i, acc)
 
         @pl.when(lax.rem(2 * i + 2, blocks) == 0)
         def _():
@@ -177,6 +193,21 @@
         return carry
 
     lax.fori_loop(0, total // 2, body, 0)
+
+    @pl.when(halved)
+    def _():
+        acc2[...] = jnp.zeros_like(acc2)
+
+        def body2(i, carry):
+            twice(total + 2 * i, acc2)
+            return carry
+
+        lax.fori_loop(0, blocks // 4, body2, 0)
+        for pair in range(8):
+            for w in range(4):
+                z = acc2[pair, w, 0:16, :half] + acc2[pair, w, 16:32, half:]
+                acc[pair, w] = jnp.concatenate([z, jnp.zeros_like(z)], axis=1)
+        flush(full)
 
 
 def predict(info, heads, position, flux):
@@ -201,11 +232,12 @@
             pltpu.VMEM((FACTORS, DEPTH, LANES), BF16),
             pltpu.VMEM((FACTORS, DEPTH, LANES), BF16),
             pltpu.VMEM((DEPTH, LANES), F32),
-            pltpu.VMEM((8, 16, DEPTH), BF16),
-            pltpu.VMEM((8, 16, DEPTH), BF16),
+            pltpu.VMEM((8, 32, DEPTH), BF16),
+            pltpu.VMEM((8, 32, DEPTH), BF16),
             pltpu.VMEM((8, 4, 16, LANES), F32),
+            pltpu.VMEM((8, 4, 32, LANES), F32),
             pltpu.VMEM((row_blocks + 1, 8, LANES), F32),
-            pltpu.VMEM((row_blocks, 48, LANES), BF16),
+            pltpu.VMEM((row_blocks, 2, 48, LANES // 2), BF16),
         ],
         compiler_params=pltpu.CompilerParams(vmem_limit_bytes=40 << 20),
         cost_estimate=pl.CostEstimate(

time: 117 us -> 99.1 us (0.85)
  starting transfers between devices: 54.5 us -> 23.7 us
  Pallas kernels: 41.8 us -> 54.4 us
    ppermute x12, starting transfers between devices: 48.9 us -> 21.1 us  [swap(): return lax.ppermute(value, axis, [(d, d ^ bits) for d in range(count)])]
    pallas_call x1, Pallas kernels: 38.1 us -> 49.9 us  [predict(): pl.pallas_call(lambda *refs: predict_kernel(blocks, *refs), out_shape=jax...]
    all_to_all x1, starting transfers between devices: 5.58 us -> 2.61 us  [local(): lax.all_to_all(norm.reshape(lines * GROUP, per_owner, 96), ('bl', 'comp')...]
  transfers between devices with their start and end apart: 13 -> 13, of which waited for: 6 -> 6; matrix products, arithmetic and copies ran while one was open for 4% -> 5% of each run, Pallas kernels for 34% -> 53%
where the time goes in v1:
time: 99.1 us; the launch traced here: 97.8 us
  Pallas kernels  54.4 us (55%)
  starting transfers between devices  23.7 us (24%)
  waiting for transfers between devices  9.68 us (10%)
  local copies, waits for them, and re-layouts  6.62 us (7%)
  between operations  1.82 us (2%)
  other arithmetic  1.68 us (2%)
    pallas_call x1, Pallas kernels, predict(): pl.pallas_call(lambda *refs: predict_kernel(blocks, *refs), out_shape=jax...  49.9 us
    ppermute x12, starting transfers between devices, swap(): return lax.ppermute(value, axis, [(d, d ^ bits) for d in range(count)])  21.1 us
    ppermute x12, waiting for transfers between devices, swap(): return lax.ppermute(value, axis, [(d, d ^ bits) for d in range(count)])  6.1 us
    unnamed x19, local copies, waits for them, and re-layouts  3.68 us
    all_to_all x1, waiting for transfers between devices, local(): lax.all_to_all(norm.reshape(lines * GROUP, per_owner, 96), ('bl', 'comp')...  3.58 us
    pallas_call x1, Pallas kernels, calibrate(): pl.pallas_call(calibrate_kernel, out_shape=(jax.ShapeDtypeStruct((GROUP,...  2.81 us
    all_to_all x1, starting transfers between devices, local(): lax.all_to_all(norm.reshape(lines * GROUP, per_owner, 96), ('bl', 'comp')...  2.61 us
  transfers between devices with their start and end apart: 13, of which 6 were waited for; matrix products, arithmetic and copies ran while one was open for 5% of the time, Pallas kernels for 53%

profile of v1, /device:TPU:0, one launch (start us, length us, event | category | flops | bytes accessed | tf_op | source)
XLA Modules:
  0.0 97.8 jit_solution(6110959104751838913)
XLA Ops:
  1.3 0.2 convert_reduce_fusion
  1.6 0.3 select_reduce_fusion
  2.1 0.8 copy-done.2
  3.1 0.6 copy-done.3
  3.8 3.0 %collective-permute-start.1 = (f32[44,256]{1,0:T(8,128)S(1)}, f32[44,256]{1,0:T(8,128)S(1)}, u32[]{:S(2)}, u32[]{:S(2)}) collective-permute-start(f32[44,256]{1,0:T(8,128)S(1)} %concatenate.40), channel_id=1, source_target_pairs={{0,2},{1,3},{2,0},{3,1},{4,6},{5,7},{6,4},{7,5},{8,10},{9,11},{10,... | collective-permute-start | bytes 135176 | tf_op jit(solution)/shard_map/ppermute | solution.py:388
  7.1 0.2 collective-permute-start.2
  7.3 0.5 copy-done
  8.1 0.1 copy.60
  8.7 0.5 pad_maximum_fusion
  9.7 0.1 reduce-precision_convert_fusion
  10.1 0.3 copy.59
  10.5 0.2 collective-permute-done.2.refs_4_.h3
  10.7 2.7 %collective-permute-start.4 = (f32[16,256]{1,0:T(8,128)S(1)}, f32[16,256]{1,0:T(8,128)S(1)}, u32[]{:S(2)}, u32[]{:S(2)}) collective-permute-start(f32[16,256]{1,0:T(8,128)S(1)} %get-tuple-element.46), channel_id=1, source_target_pairs={{0,16},{4,20},{8,24},{12,28},{16,0},{20,4},{24,8},{28,12},{1,17},{... | collective-permute-start | bytes 49160 | tf_op jit(solution)/shard_map/ppermute | solution.py:388
  13.4 1.6 %collective-permute-start.3 = (f32[16,256]{1,0:T(8,128)S(1)}, f32[16,256]{1,0:T(8,128)S(1)}, u32[]{:S(2)}, u32[]{:S(2)}) collective-permute-start(f32[16,256]{1,0:T(8,128)S(1)} %get-tuple-element.46), channel_id=1, source_target_pairs={{0,8},{4,12},{8,0},{12,4},{16,24},{20,28},{24,16},{28,20},{1,9},{5... | collective-permute-start | bytes 49160 | tf_op jit(solution)/shard_map/ppermute | solution.py:388
  14.9 0.2 collective-permute-start.5
  15.2 49.9 %predict.1 = f32[2,2,4,4,8,256]{5,4,3,2,1,0:T(8,128)S(1)} custom-call(s32[2]{0:T(128)S(1)} %pad_add_fusion.refs_0_.info_ref, f32[44,256]{1,0:T(8,128)S(1)} %concatenate.38.refs_1_.h0, f32[44,256]{1,0:T(8,128)S(1)} %collective-permute-done.refs_2_.h1, f32[44,256]{1,0:T(8,128)S(1)} %collective-permute-done.1.refs_3_.h2, ...), custom_call_target="tpu_custom_call" | custom-call | flops 2147483648 | bytes 4194304 | tf_op jit(solution)/shard_map/predict/pallas_call | solution.py:226
  65.3 9.9 %collective-permute-start.6 = (f32[4,16,256]{2,1,0:T(8,128)S(1)}, f32[4,16,256]{2,1,0:T(8,128)S(1)}, u32[]{:S(2)}, u32[]{:S(2)}) collective-permute-start(f32[4,16,256]{2,1,0:T(8,128)S(1)} %get-tuple-element.44), channel_id=1, source_target_pairs={{0,4},{4,0},{8,12},{12,8},{16,20},{20,16},{24,28},{28,24},{1,5},{5... | collective-permute-start | bytes 196616 | tf_op jit(solution)/shard_map/ppermute | solution.py:388
  75.2 1.4 %collective-permute-start.8 = (f32[4,4,8,256]{3,2,1,0:T(8,128)S(1)}, f32[4,4,8,256]{3,2,1,0:T(8,128)S(1)}, u32[]{:S(2)}, u32[]{:S(2)}) collective-permute-start(f32[4,4,8,256]{3,2,1,0:T(8,128)S(1)} %fusion.3), channel_id=1, source_target_pairs={{0,2},{1,3},{2,0},{3,1},{4,6},{5,7},{6,4},{7,5},{8,10},{9,11},{10,... | collective-permute-start | bytes 393224 | tf_op jit(solution)/shard_map/ppermute | solution.py:388
  76.6 1.3 %collective-permute-done.6 = f32[4,16,256]{2,1,0:T(8,128)S(1)} collective-permute-done((f32[4,16,256]{2,1,0:T(8,128)S(1)}, f32[4,16,256]{2,1,0:T(8,128)S(1)}, u32[]{:S(2)}, u32[]{:S(2)}) %collective-permute-start.6) | collective-permute-done | bytes 65568 | tf_op jit(solution)/shard_map/ppermute | solution.py:388
  78.0 0.3 reshape.154
  78.3 0.3 copy.67
  78.8 1.6 %prepare.1 = (f32[5,32,256]{2,1,0:T(8,128)S(1)}, f32[5,8,256]{2,1,0:T(8,128)S(1)}, f32[4,2,16,256]{3,2,1,0:T(8,128)S(1)}) custom-call(s32[2]{0:T(128)S(1)} %pad_add_fusion.refs_0_.info_ref, f32[44,256]{1,0:T(8,128)S(1)} %concatenate.38.refs_1_.h0, f32[44,256]{1,0:T(8,128)S(1)} %collective-permute-done.refs_2_.h1, ...), custom_call_target="tpu_custom_call" | custom-call | flops 1073741824 | bytes 1048576 | tf_op jit(solution)/shard_map/prepare/pallas_call | solution.py:352
  80.4 0.5 collective-permute-done.8.far_ref
  80.9 2.8 %calibrate.1 = (f32[4,32,256]{2,1,0:T(8,128)S(1)}, f32[512,96]{1,0:T(8,128)}) custom-call(s32[2]{0:T(128)S(1)} %pad_add_fusion.refs_0_.info_ref, f32[44,256]{1,0:T(8,128)S(1)} %concatenate.38.refs_1_.h0, f32[44,256]{1,0:T(8,128)S(1)} %collective-permute-done.refs_2_.h1, f32[44,256]{1,0:T(8,128)S(1)} %collective-permute-done.1.refs_3_.h2, ...), custom_call_target="tpu_custom_call" | custom-call | tf_op jit(solution)/shard_map/calibrate/pallas_call | solution.py:369
  83.7 2.6 %all-to-all-start = ((f32[32,16,96]{2,1,0:T(8,128)}), f32[32,16,96]{2,1,0:T(8,128)S(1)}, u32[]{:S(2)}, u32[]{:S(2)}) async-start(f32[32,16,96]{2,1,0:T(8,128)} %bitcast.35), calls=%async_computation | async-start | bytes 524288 | tf_op jit(solution)/shard_map/all_to_all | solution.py:446
  86.3 0.3 collective-permute-start.11
  86.7 1.7 %collective-permute-start.10 = (f32[32,256]{1,0:T(8,128)S(1)}, f32[32,256]{1,0:T(8,128)S(1)}, u32[]{:S(2)}, u32[]{:S(2)}) collective-permute-start(f32[32,256]{1,0:T(8,128)S(1)} %get-tuple-element.33), channel_id=1, source_target_pairs={{0,2},{1,3},{2,0},{3,1},{4,6},{5,7},{6,4},{7,5},{8,10},{9,11},{10,... | collective-permute-start | bytes 98312 | tf_op jit(solution)/shard_map/ppermute | solution.py:388
  88.4 2.5 %collective-permute-done.10 = f32[32,256]{1,0:T(8,128)S(1)} collective-permute-done((f32[32,256]{1,0:T(8,128)S(1)}, f32[32,256]{1,0:T(8,128)S(1)}, u32[]{:S(2)}, u32[]{:S(2)}) %collective-permute-start.10) | collective-permute-done | bytes 32800 | tf_op jit(solution)/shard_map/ppermute | solution.py:388
  90.9 1.5 %collective-permute-done.9 = f32[32,256]{1,0:T(8,128)S(1)} collective-permute-done((f32[32,256]{1,0:T(8,128)S(1)}, f32[32,256]{1,0:T(8,128)S(1)}, u32[]{:S(2)}, u32[]{:S(2)}) %collective-permute-start.9) | collective-permute-done | bytes 32800 | tf_op jit(solution)/shard_map/ppermute | solution.py:388
  92.6 0.8 copy.75
  93.4 3.6 %all-to-all-done = f32[32,16,96]{2,1,0:T(8,128)S(1)} async-done(((f32[32,16,96]{2,1,0:T(8,128)}), f32[32,16,96]{2,1,0:T(8,128)S(1)}, u32[]{:S(2)}, u32[]{:S(2)}) %all-to-all-start) | async-done | bytes 196640 | tf_op jit(solution)/shard_map/all_to_all | solution.py:446
  97.1 0.7 copy.76
  (83 shorter events, 2.9 us)
Async XLA Ops:
  0.6 1.0 copy-start.6
  0.6 0.7 copy-start.4
  0.7 1.2 %copy-start.5 = (f32[16,256]{1,0:T(8,128)S(1)}, f32[16,256]{1,0:T(8,128)}, u32[]{:S(2)}) copy-start(f32[16,256]{1,0:T(8,128)} %param.13) | copy-start | bytes 49156
  2.0 0.9 copy-start.2
  3.0 0.7 copy-start.3
  3.1 5.0 %copy-start.1 = (f32[4,16,2048]{2,1,0:T(8,128)S(1)}, f32[4,16,2048]{2,1,0:T(8,128)}, u32[]{:S(2)}) copy-start(f32[4,16,2048]{2,1,0:T(8,128)} %param.12) | copy-start | bytes 1572868
  3.8 6.7 %collective-permute-start.1 = (f32[44,256]{1,0:T(8,128)S(1)}, f32[44,256]{1,0:T(8,128)S(1)}, u32[]{:S(2)}, u32[]{:S(2)}) collective-permute-start(f32[44,256]{1,0:T(8,128)S(1)} %concatenate.40), channel_id=1, source_target_pairs={{0,2},{1,3},{2,0},{3,1},{4,6},{5,7},{6,4},{7,5},{8,10},{9,11},{10,... | collective-permute-start | bytes 135176 | tf_op jit(solution)/shard_map/ppermute | solution.py:388
  6.9 3.6 %collective-permute-start = (f32[44,256]{1,0:T(8,128)S(1)}, f32[44,256]{1,0:T(8,128)S(1)}, u32[]{:S(2)}, u32[]{:S(2)}) collective-permute-start(f32[44,256]{1,0:T(8,128)S(1)} %concatenate.39), channel_id=1, source_target_pairs={{0,1},{1,0},{2,3},{3,2},{4,5},{5,4},{6,7},{7,6},{8,9},{9,8},{10,11... | collective-permute-start | bytes 135176 | tf_op jit(solution)/shard_map/ppermute | solution.py:388
  7.1 0.7 copy-start
  7.1 3.6 %collective-permute-start.2 = (f32[44,256]{1,0:T(8,128)S(1)}, f32[44,256]{1,0:T(8,128)S(1)}, u32[]{:S(2)}, u32[]{:S(2)}) collective-permute-start(f32[44,256]{1,0:T(8,128)S(1)} %concatenate.41), channel_id=1, source_target_pairs={{0,3},{1,2},{2,1},{3,0},{4,7},{5,6},{6,5},{7,4},{8,11},{9,10},{10,... | collective-permute-start | bytes 135176 | tf_op jit(solution)/shard_map/ppermute | solution.py:388
  10.7 54.5 %collective-permute-start.4 = (f32[16,256]{1,0:T(8,128)S(1)}, f32[16,256]{1,0:T(8,128)S(1)}, u32[]{:S(2)}, u32[]{:S(2)}) collective-permute-start(f32[16,256]{1,0:T(8,128)S(1)} %get-tuple-element.46), channel_id=1, source_target_pairs={{0,16},{4,20},{8,24},{12,28},{16,0},{20,4},{24,8},{28,12},{1,17},{... | collective-permute-start | bytes 49160 | tf_op jit(solution)/shard_map/ppermute | solution.py:388
  13.4 51.8 %collective-permute-start.3 = (f32[16,256]{1,0:T(8,128)S(1)}, f32[16,256]{1,0:T(8,128)S(1)}, u32[]{:S(2)}, u32[]{:S(2)}) collective-permute-start(f32[16,256]{1,0:T(8,128)S(1)} %get-tuple-element.46), channel_id=1, source_target_pairs={{0,8},{4,12},{8,0},{12,4},{16,24},{20,28},{24,16},{28,20},{1,9},{5... | collective-permute-start | bytes 49160 | tf_op jit(solution)/shard_map/ppermute | solution.py:388
  14.9 50.3 %collective-permute-start.5 = (f32[16,256]{1,0:T(8,128)S(1)}, f32[16,256]{1,0:T(8,128)S(1)}, u32[]{:S(2)}, u32[]{:S(2)}) collective-permute-start(f32[16,256]{1,0:T(8,128)S(1)} %get-tuple-element.46), channel_id=1, source_target_pairs={{0,24},{4,28},{8,16},{12,20},{16,8},{20,12},{24,0},{28,4},{1,25},{... | collective-permute-start | bytes 49160 | tf_op jit(solution)/shard_map/ppermute | solution.py:388
  65.1 10.1 %collective-permute-start.7 = (f32[2,4,4,8,256]{4,3,2,1,0:T(8,128)S(1)}, f32[2,4,4,8,256]{4,3,2,1,0:T(8,128)S(1)}, u32[]{:S(2)}, u32[]{:S(2)}) collective-permute-start(f32[2,4,4,8,256]{4,3,2,1,0:T(8,128)S(1)} %slice_bitcast_fusion), channel_id=1, source_target_pairs={{0,1},{1,0},{2,3},{3,2},{4,5},{5,4},{6,7},{7,6},{8,9},{9,8},{10,11... | collective-permute-start | bytes 786440 | tf_op jit(solution)/shard_map/ppermute | solution.py:388
  65.3 12.7 %collective-permute-start.6 = (f32[4,16,256]{2,1,0:T(8,128)S(1)}, f32[4,16,256]{2,1,0:T(8,128)S(1)}, u32[]{:S(2)}, u32[]{:S(2)}) collective-permute-start(f32[4,16,256]{2,1,0:T(8,128)S(1)} %get-tuple-element.44), channel_id=1, source_target_pairs={{0,4},{4,0},{8,12},{12,8},{16,20},{20,16},{24,28},{28,24},{1,5},{5... | collective-permute-start | bytes 196616 | tf_op jit(solution)/shard_map/ppermute | solution.py:388
  75.2 5.7 %collective-permute-start.8 = (f32[4,4,8,256]{3,2,1,0:T(8,128)S(1)}, f32[4,4,8,256]{3,2,1,0:T(8,128)S(1)}, u32[]{:S(2)}, u32[]{:S(2)}) collective-permute-start(f32[4,4,8,256]{3,2,1,0:T(8,128)S(1)} %fusion.3), channel_id=1, source_target_pairs={{0,2},{1,3},{2,0},{3,1},{4,6},{5,7},{6,4},{7,5},{8,10},{9,11},{10,... | collective-permute-start | bytes 393224 | tf_op jit(solution)/shard_map/ppermute | solution.py:388
  83.7 13.2 %all-to-all-start = ((f32[32,16,96]{2,1,0:T(8,128)}), f32[32,16,96]{2,1,0:T(8,128)S(1)}, u32[]{:S(2)}, u32[]{:S(2)}) async-start(f32[32,16,96]{2,1,0:T(8,128)} %bitcast.35), calls=%async_computation | async-start | bytes 524288 | tf_op jit(solution)/shard_map/all_to_all | solution.py:446
  86.3 2.0 %collective-permute-start.11 = (f32[32,256]{1,0:T(8,128)S(1)}, f32[32,256]{1,0:T(8,128)S(1)}, u32[]{:S(2)}, u32[]{:S(2)}) collective-permute-start(f32[32,256]{1,0:T(8,128)S(1)} %get-tuple-element.32), channel_id=1, source_target_pairs={{0,1},{1,0},{2,3},{3,2},{4,5},{5,4},{6,7},{7,6},{8,9},{9,8},{10,11... | collective-permute-start | bytes 98312 | tf_op jit(solution)/shard_map/ppermute | solution.py:388
  86.7 4.2 %collective-permute-start.10 = (f32[32,256]{1,0:T(8,128)S(1)}, f32[32,256]{1,0:T(8,128)S(1)}, u32[]{:S(2)}, u32[]{:S(2)}) collective-permute-start(f32[32,256]{1,0:T(8,128)S(1)} %get-tuple-element.33), channel_id=1, source_target_pairs={{0,2},{1,3},{2,0},{3,1},{4,6},{5,7},{6,4},{7,5},{8,10},{9,11},{10,... | collective-permute-start | bytes 98312 | tf_op jit(solution)/shard_map/ppermute | solution.py:388
  88.3 4.1 %collective-permute-start.9 = (f32[32,256]{1,0:T(8,128)S(1)}, f32[32,256]{1,0:T(8,128)S(1)}, u32[]{:S(2)}, u32[]{:S(2)}) collective-permute-start(f32[32,256]{1,0:T(8,128)S(1)} %get-tuple-element.34), channel_id=1, source_target_pairs={{0,3},{1,2},{2,1},{3,0},{4,7},{5,6},{6,5},{7,4},{8,11},{9,10},{10,... | collective-permute-start | bytes 98312 | tf_op jit(solution)/shard_map/ppermute | solution.py:388

commit v2 on v1

--- a/solution.py
+++ b/solution.py
@@ -98,7 +98,6 @@
     halved = (rest_rows > 0) & (rest_rows <= half)
     full = lax.div(live + half - 1, LANES)
     total = full * blocks
-    last = total + jnp.where(halved, blocks // 2, 0) - 1
     rows_ref[...] = jnp.zeros_like(rows_ref)
     for b, head in enumerate((h0, h1, h2, h3)):
         place(rows_ref, head[0:8], starts[b], counts[b])
@@ -108,21 +107,24 @@
             part = rest.astype(BF16).astype(F32)
             parts.append(part)
             rest = rest - part
-        u = jnp.concatenate([parts[i] for i, _ in TERMS], axis=0).astype(BF16)
-        u_ref[row, 0] = u[:, :half]
-        u_ref[row, 1] = u[:, half:]
+        u_ref[row] = jnp.concatenate([parts[i] for i, _ in TERMS], axis=0).astype(BF16)
+
+    def depth(block):
+        return pl.ds(pl.multiple_of(block * DEPTH, DEPTH), DEPTH)
 
     def begin(index, table):
-        index = jnp.minimum(index, last)
-        extra = index - total
-        pair = extra >= 0
-        row = jnp.where(pair, full, lax.div(index, blocks))
-        left = jnp.where(pair, 2 * extra, lax.rem(index, blocks))
-        right = jnp.where(pair, left + 1, left)
-        for side, block in enumerate((left, right)):
-            comps = pl.ds(pl.multiple_of(block * DEPTH, DEPTH), DEPTH)
-            u = u_ref[row, jnp.where(pair, 0, side)]
-            tt[:, side * half : side * half + half] = jnp.dot(l_ref[comps, :], u, preferred_element_type=F32)
+        index = jnp.clip(index, 0, jnp.maximum(total - 1, 0))
+        row, block = lax.div(index, blocks), lax.rem(index, blocks)
+        tt[...] = jnp.dot(l_ref[depth(block), :], u_ref[row], preferred_element_type=F32)
+        table[:, 0:16] = tab_ref[block]
+
+    def begin_halved(index, table):
+        index = jnp.minimum(index, blocks // 2 - 1)
+        for side in range(2):
+            block = 2 * index + side
+            tt[:, side * half : side * half + half] = jnp.dot(
+                l_ref[depth(block), :], u_ref[full, :, :half], preferred_element_type=F32
+            )
             table[:, 16 * side : 16 * side + 16] = tab_ref[block]
 
     def strips(f):
@@ -173,18 +175,22 @@
 
     o_ref[...] = jnp.zeros_like(o_ref)
     acc[...] = jnp.zeros_like(acc)
-    begin(0, ta)
-    for _ in strips(fa):
-        pass
-
-    def twice(first, into):
-        begin(first + 1, tb)
+
+    def first(start):
+        start(0, ta)
+        for _ in strips(fa):
+            pass
+
+    def twice(start, index, into):
+        start(index + 1, tb)
         step(fa, fb, ta, into)
-        begin(first + 2, ta)
+        start(index + 2, ta)
         step(fb, fa, tb, into)
 
+    first(begin)
+
     def body(i, carry):
-        twice(2 * i, acc)
+        twice(begin, 2 * i, acc)
 
         @pl.when(lax.rem(2 * i + 2, blocks) == 0)
         def _():
@@ -197,9 +203,10 @@
     @pl.when(halved)
     def _():
         acc2[...] = jnp.zeros_like(acc2)
+        first(begin_halved)
 
         def body2(i, carry):
-            twice(total + 2 * i, acc2)
+            twice(begin_halved, 2 * i, acc2)
             return carry
 
         lax.fori_loop(0, blocks // 4, body2, 0)
@@ -237,7 +244,7 @@
             pltpu.VMEM((8, 4, 16, LANES), F32),
             pltpu.VMEM((8, 4, 32, LANES), F32),
             pltpu.VMEM((row_blocks + 1, 8, LANES), F32),
-            pltpu.VMEM((row_blocks, 2, 48, LANES // 2), BF16),
+            pltpu.VMEM((row_blocks, 48, LANES), BF16),
         ],
         compiler_params=pltpu.CompilerParams(vmem_limit_bytes=40 << 20),
         cost_estimate=pl.CostEstimate(

time: 99.1 us -> 99.7 us (level)
  starting transfers between devices: 23.7 us -> 36.9 us
  Pallas kernels: 54.4 us -> 42.4 us
    all_to_all x1, starting transfers between devices: 2.61 us -> 24.2 us  [local(): lax.all_to_all(norm.reshape(lines * GROUP, per_owner, 96), ('bl', 'comp')...]
    pallas_call x1, Pallas kernels: 49.9 us -> 38.6 us  [predict(): pl.pallas_call(lambda *refs: predict_kernel(blocks, *refs), out_shape=jax...]
    ppermute x12, starting transfers between devices: 21.1 us -> 12.7 us  [swap(): return lax.ppermute(value, axis, [(d, d ^ bits) for d in range(count)])]
  transfers between devices with their start and end apart: 13 -> 13, of which waited for: 6 -> 6; matrix products, arithmetic and copies ran while one was open for 5% -> 5% of each run, Pallas kernels for 53% -> 40%
where the time goes in v2:
time: 99.7 us; the launch traced here: 99.4 us
  Pallas kernels  42.4 us (43%)
  starting transfers between devices  36.9 us (37%)
  waiting for transfers between devices  9.96 us (10%)
  local copies, waits for them, and re-layouts  6.62 us (7%)
  between operations  1.82 us (2%)
  other arithmetic  1.68 us (2%)
    pallas_call x1, Pallas kernels, predict(): pl.pallas_call(lambda *refs: predict_kernel(blocks, *refs), out_shape=jax...  38.6 us
    all_to_all x1, starting transfers between devices, local(): lax.all_to_all(norm.reshape(lines * GROUP, per_owner, 96), ('bl', 'comp')...  24.2 us
    ppermute x12, starting transfers between devices, swap(): return lax.ppermute(value, axis, [(d, d ^ bits) for d in range(count)])  12.7 us
    ppermute x12, waiting for transfers between devices, swap(): return lax.ppermute(value, axis, [(d, d ^ bits) for d in range(count)])  6.38 us
    unnamed x19, local copies, waits for them, and re-layouts  3.68 us
    all_to_all x1, waiting for transfers between devices, local(): lax.all_to_all(norm.reshape(lines * GROUP, per_owner, 96), ('bl', 'comp')...  3.57 us
    pallas_call x1, Pallas kernels, calibrate(): pl.pallas_call(calibrate_kernel, out_shape=(jax.ShapeDtypeStruct((GROUP,...  2.4 us
  transfers between devices with their start and end apart: 13, of which 6 were waited for; matrix products, arithmetic and copies ran while one was open for 5% of the time, Pallas kernels for 40%

profile of v2, /device:TPU:0, one launch (start us, length us, event | category | flops | bytes accessed | tf_op | source)
XLA Modules:
  0.0 99.4 jit_solution(3090827226356022607)
XLA Ops:
  1.3 0.2 convert_reduce_fusion
  1.6 0.3 select_reduce_fusion
  2.1 0.8 copy-done.2
  3.1 0.6 copy-done.3
  3.8 3.0 %collective-permute-start.1 = (f32[44,256]{1,0:T(8,128)S(1)}, f32[44,256]{1,0:T(8,128)S(1)}, u32[]{:S(2)}, u32[]{:S(2)}) collective-permute-start(f32[44,256]{1,0:T(8,128)S(1)} %concatenate.40), channel_id=1, source_target_pairs={{0,2},{1,3},{2,0},{3,1},{4,6},{5,7},{6,4},{7,5},{8,10},{9,11},{10,... | collective-permute-start | bytes 135176 | tf_op jit(solution)/shard_map/ppermute | solution.py:395
  7.1 0.2 collective-permute-start.2
  7.3 0.5 copy-done
  8.1 0.1 copy.60
  8.7 0.5 pad_maximum_fusion
  9.7 0.1 reduce-precision_convert_fusion
  10.1 0.3 copy.59
  10.5 0.2 collective-permute-done.2.refs_4_.h3
  10.7 2.7 %collective-permute-start.4 = (f32[16,256]{1,0:T(8,128)S(1)}, f32[16,256]{1,0:T(8,128)S(1)}, u32[]{:S(2)}, u32[]{:S(2)}) collective-permute-start(f32[16,256]{1,0:T(8,128)S(1)} %get-tuple-element.46), channel_id=1, source_target_pairs={{0,16},{4,20},{8,24},{12,28},{16,0},{20,4},{24,8},{28,12},{1,17},{... | collective-permute-start | bytes 49160 | tf_op jit(solution)/shard_map/ppermute | solution.py:395
  13.4 1.6 %collective-permute-start.3 = (f32[16,256]{1,0:T(8,128)S(1)}, f32[16,256]{1,0:T(8,128)S(1)}, u32[]{:S(2)}, u32[]{:S(2)}) collective-permute-start(f32[16,256]{1,0:T(8,128)S(1)} %get-tuple-element.46), channel_id=1, source_target_pairs={{0,8},{4,12},{8,0},{12,4},{16,24},{20,28},{24,16},{28,20},{1,9},{5... | collective-permute-start | bytes 49160 | tf_op jit(solution)/shard_map/ppermute | solution.py:395
  14.9 0.2 collective-permute-start.5
  15.2 38.6 %predict.1 = f32[2,2,4,4,8,256]{5,4,3,2,1,0:T(8,128)S(1)} custom-call(s32[2]{0:T(128)S(1)} %pad_add_fusion.refs_0_.info_ref, f32[44,256]{1,0:T(8,128)S(1)} %concatenate.38.refs_1_.h0, f32[44,256]{1,0:T(8,128)S(1)} %collective-permute-done.refs_2_.h1, f32[44,256]{1,0:T(8,128)S(1)} %collective-permute-done.1.refs_3_.h2, ...), custom_call_target="tpu_custom_call" | custom-call | flops 2147483648 | bytes 4194304 | tf_op jit(solution)/shard_map/predict/pallas_call | solution.py:233
  54.0 1.6 %collective-permute-start.6 = (f32[4,16,256]{2,1,0:T(8,128)S(1)}, f32[4,16,256]{2,1,0:T(8,128)S(1)}, u32[]{:S(2)}, u32[]{:S(2)}) collective-permute-start(f32[4,16,256]{2,1,0:T(8,128)S(1)} %get-tuple-element.44), channel_id=1, source_target_pairs={{0,4},{4,0},{8,12},{12,8},{16,20},{20,16},{24,28},{28,24},{1,5},{5... | collective-permute-start | bytes 196616 | tf_op jit(solution)/shard_map/ppermute | solution.py:395
  55.6 1.4 %collective-permute-start.8 = (f32[4,4,8,256]{3,2,1,0:T(8,128)S(1)}, f32[4,4,8,256]{3,2,1,0:T(8,128)S(1)}, u32[]{:S(2)}, u32[]{:S(2)}) collective-permute-start(f32[4,4,8,256]{3,2,1,0:T(8,128)S(1)} %fusion.3), channel_id=1, source_target_pairs={{0,2},{1,3},{2,0},{3,1},{4,6},{5,7},{6,4},{7,5},{8,10},{9,11},{10,... | collective-permute-start | bytes 393224 | tf_op jit(solution)/shard_map/ppermute | solution.py:395
  57.0 1.6 %collective-permute-done.6 = f32[4,16,256]{2,1,0:T(8,128)S(1)} collective-permute-done((f32[4,16,256]{2,1,0:T(8,128)S(1)}, f32[4,16,256]{2,1,0:T(8,128)S(1)}, u32[]{:S(2)}, u32[]{:S(2)}) %collective-permute-start.6) | collective-permute-done | bytes 65568 | tf_op jit(solution)/shard_map/ppermute | solution.py:395
  58.6 0.3 reshape.154
  58.9 0.3 copy.67
  59.4 1.4 %prepare.1 = (f32[5,32,256]{2,1,0:T(8,128)S(1)}, f32[5,8,256]{2,1,0:T(8,128)S(1)}, f32[4,2,16,256]{3,2,1,0:T(8,128)S(1)}) custom-call(s32[2]{0:T(128)S(1)} %pad_add_fusion.refs_0_.info_ref, f32[44,256]{1,0:T(8,128)S(1)} %concatenate.38.refs_1_.h0, f32[44,256]{1,0:T(8,128)S(1)} %collective-permute-done.refs_2_.h1, ...), custom_call_target="tpu_custom_call" | custom-call | flops 1073741824 | bytes 1048576 | tf_op jit(solution)/shard_map/prepare/pallas_call | solution.py:359
  60.7 0.5 collective-permute-done.8.far_ref
  61.3 2.4 %calibrate.1 = (f32[4,32,256]{2,1,0:T(8,128)S(1)}, f32[512,96]{1,0:T(8,128)}) custom-call(s32[2]{0:T(128)S(1)} %pad_add_fusion.refs_0_.info_ref, f32[44,256]{1,0:T(8,128)S(1)} %concatenate.38.refs_1_.h0, f32[44,256]{1,0:T(8,128)S(1)} %collective-permute-done.refs_2_.h1, f32[44,256]{1,0:T(8,128)S(1)} %collective-permute-done.1.refs_3_.h2, ...), custom_call_target="tpu_custom_call" | custom-call | tf_op jit(solution)/shard_map/calibrate/pallas_call | solution.py:376
  63.7 24.2 %all-to-all-start = ((f32[32,16,96]{2,1,0:T(8,128)}), f32[32,16,96]{2,1,0:T(8,128)S(1)}, u32[]{:S(2)}, u32[]{:S(2)}) async-start(f32[32,16,96]{2,1,0:T(8,128)} %bitcast.35), calls=%async_computation | async-start | bytes 524288 | tf_op jit(solution)/shard_map/all_to_all | solution.py:453
  87.9 0.3 collective-permute-start.11
  88.2 1.7 %collective-permute-start.10 = (f32[32,256]{1,0:T(8,128)S(1)}, f32[32,256]{1,0:T(8,128)S(1)}, u32[]{:S(2)}, u32[]{:S(2)}) collective-permute-start(f32[32,256]{1,0:T(8,128)S(1)} %get-tuple-element.33), channel_id=1, source_target_pairs={{0,2},{1,3},{2,0},{3,1},{4,6},{5,7},{6,4},{7,5},{8,10},{9,11},{10,... | collective-permute-start | bytes 98312 | tf_op jit(solution)/shard_map/ppermute | solution.py:395
  89.9 2.5 %collective-permute-done.10 = f32[32,256]{1,0:T(8,128)S(1)} collective-permute-done((f32[32,256]{1,0:T(8,128)S(1)}, f32[32,256]{1,0:T(8,128)S(1)}, u32[]{:S(2)}, u32[]{:S(2)}) %collective-permute-start.10) | collective-permute-done | bytes 32800 | tf_op jit(solution)/shard_map/ppermute | solution.py:395
  92.4 1.5 %collective-permute-done.9 = f32[32,256]{1,0:T(8,128)S(1)} collective-permute-done((f32[32,256]{1,0:T(8,128)S(1)}, f32[32,256]{1,0:T(8,128)S(1)}, u32[]{:S(2)}, u32[]{:S(2)}) %collective-permute-start.9) | collective-permute-done | bytes 32800 | tf_op jit(solution)/shard_map/ppermute | solution.py:395
  94.1 0.8 copy.75
  94.9 3.6 %all-to-all-done = f32[32,16,96]{2,1,0:T(8,128)S(1)} async-done(((f32[32,16,96]{2,1,0:T(8,128)}), f32[32,16,96]{2,1,0:T(8,128)S(1)}, u32[]{:S(2)}, u32[]{:S(2)}) %all-to-all-start) | async-done | bytes 196640 | tf_op jit(solution)/shard_map/all_to_all | solution.py:453
  98.7 0.7 copy.76
  (83 shorter events, 2.9 us)
Async XLA Ops:
  0.6 1.0 copy-start.6
  0.6 0.7 copy-start.4
  0.7 1.2 %copy-start.5 = (f32[16,256]{1,0:T(8,128)S(1)}, f32[16,256]{1,0:T(8,128)}, u32[]{:S(2)}) copy-start(f32[16,256]{1,0:T(8,128)} %param.13) | copy-start | bytes 49156
  2.0 0.9 copy-start.2
  3.0 0.7 copy-start.3
  3.1 5.0 %copy-start.1 = (f32[4,16,2048]{2,1,0:T(8,128)S(1)}, f32[4,16,2048]{2,1,0:T(8,128)}, u32[]{:S(2)}) copy-start(f32[4,16,2048]{2,1,0:T(8,128)} %param.12) | copy-start | bytes 1572868
  3.8 6.7 %collective-permute-start.1 = (f32[44,256]{1,0:T(8,128)S(1)}, f32[44,256]{1,0:T(8,128)S(1)}, u32[]{:S(2)}, u32[]{:S(2)}) collective-permute-start(f32[44,256]{1,0:T(8,128)S(1)} %concatenate.40), channel_id=1, source_target_pairs={{0,2},{1,3},{2,0},{3,1},{4,6},{5,7},{6,4},{7,5},{8,10},{9,11},{10,... | collective-permute-start | bytes 135176 | tf_op jit(solution)/shard_map/ppermute | solution.py:395
  6.9 3.6 %collective-permute-start = (f32[44,256]{1,0:T(8,128)S(1)}, f32[44,256]{1,0:T(8,128)S(1)}, u32[]{:S(2)}, u32[]{:S(2)}) collective-permute-start(f32[44,256]{1,0:T(8,128)S(1)} %concatenate.39), channel_id=1, source_target_pairs={{0,1},{1,0},{2,3},{3,2},{4,5},{5,4},{6,7},{7,6},{8,9},{9,8},{10,11... | collective-permute-start | bytes 135176 | tf_op jit(solution)/shard_map/ppermute | solution.py:395
  7.1 0.7 copy-start
  7.1 3.6 %collective-permute-start.2 = (f32[44,256]{1,0:T(8,128)S(1)}, f32[44,256]{1,0:T(8,128)S(1)}, u32[]{:S(2)}, u32[]{:S(2)}) collective-permute-start(f32[44,256]{1,0:T(8,128)S(1)} %concatenate.41), channel_id=1, source_target_pairs={{0,3},{1,2},{2,1},{3,0},{4,7},{5,6},{6,5},{7,4},{8,11},{9,10},{10,... | collective-permute-start | bytes 135176 | tf_op jit(solution)/shard_map/ppermute | solution.py:395
  10.7 43.2 %collective-permute-start.4 = (f32[16,256]{1,0:T(8,128)S(1)}, f32[16,256]{1,0:T(8,128)S(1)}, u32[]{:S(2)}, u32[]{:S(2)}) collective-permute-start(f32[16,256]{1,0:T(8,128)S(1)} %get-tuple-element.46), channel_id=1, source_target_pairs={{0,16},{4,20},{8,24},{12,28},{16,0},{20,4},{24,8},{28,12},{1,17},{... | collective-permute-start | bytes 49160 | tf_op jit(solution)/shard_map/ppermute | solution.py:395
  13.4 40.6 %collective-permute-start.3 = (f32[16,256]{1,0:T(8,128)S(1)}, f32[16,256]{1,0:T(8,128)S(1)}, u32[]{:S(2)}, u32[]{:S(2)}) collective-permute-start(f32[16,256]{1,0:T(8,128)S(1)} %get-tuple-element.46), channel_id=1, source_target_pairs={{0,8},{4,12},{8,0},{12,4},{16,24},{20,28},{24,16},{28,20},{1,9},{5... | collective-permute-start | bytes 49160 | tf_op jit(solution)/shard_map/ppermute | solution.py:395
  14.9 39.0 %collective-permute-start.5 = (f32[16,256]{1,0:T(8,128)S(1)}, f32[16,256]{1,0:T(8,128)S(1)}, u32[]{:S(2)}, u32[]{:S(2)}) collective-permute-start(f32[16,256]{1,0:T(8,128)S(1)} %get-tuple-element.46), channel_id=1, source_target_pairs={{0,24},{4,28},{8,16},{12,20},{16,8},{20,12},{24,0},{28,4},{1,25},{... | collective-permute-start | bytes 49160 | tf_op jit(solution)/shard_map/ppermute | solution.py:395
  53.8 1.7 %collective-permute-start.7 = (f32[2,4,4,8,256]{4,3,2,1,0:T(8,128)S(1)}, f32[2,4,4,8,256]{4,3,2,1,0:T(8,128)S(1)}, u32[]{:S(2)}, u32[]{:S(2)}) collective-permute-start(f32[2,4,4,8,256]{4,3,2,1,0:T(8,128)S(1)} %slice_bitcast_fusion), channel_id=1, source_target_pairs={{0,1},{1,0},{2,3},{3,2},{4,5},{5,4},{6,7},{7,6},{8,9},{9,8},{10,11... | collective-permute-start | bytes 786440 | tf_op jit(solution)/shard_map/ppermute | solution.py:395
  54.0 4.6 %collective-permute-start.6 = (f32[4,16,256]{2,1,0:T(8,128)S(1)}, f32[4,16,256]{2,1,0:T(8,128)S(1)}, u32[]{:S(2)}, u32[]{:S(2)}) collective-permute-start(f32[4,16,256]{2,1,0:T(8,128)S(1)} %get-tuple-element.44), channel_id=1, source_target_pairs={{0,4},{4,0},{8,12},{12,8},{16,20},{20,16},{24,28},{28,24},{1,5},{5... | collective-permute-start | bytes 196616 | tf_op jit(solution)/shard_map/ppermute | solution.py:395
  55.6 5.7 %collective-permute-start.8 = (f32[4,4,8,256]{3,2,1,0:T(8,128)S(1)}, f32[4,4,8,256]{3,2,1,0:T(8,128)S(1)}, u32[]{:S(2)}, u32[]{:S(2)}) collective-permute-start(f32[4,4,8,256]{3,2,1,0:T(8,128)S(1)} %fusion.3), channel_id=1, source_target_pairs={{0,2},{1,3},{2,0},{3,1},{4,6},{5,7},{6,4},{7,5},{8,10},{9,11},{10,... | collective-permute-start | bytes 393224 | tf_op jit(solution)/shard_map/ppermute | solution.py:395
  63.7 34.8 %all-to-all-start = ((f32[32,16,96]{2,1,0:T(8,128)}), f32[32,16,96]{2,1,0:T(8,128)S(1)}, u32[]{:S(2)}, u32[]{:S(2)}) async-start(f32[32,16,96]{2,1,0:T(8,128)} %bitcast.35), calls=%async_computation | async-start | bytes 524288 | tf_op jit(solution)/shard_map/all_to_all | solution.py:453
  87.9 2.0 %collective-permute-start.11 = (f32[32,256]{1,0:T(8,128)S(1)}, f32[32,256]{1,0:T(8,128)S(1)}, u32[]{:S(2)}, u32[]{:S(2)}) collective-permute-start(f32[32,256]{1,0:T(8,128)S(1)} %get-tuple-element.32), channel_id=1, source_target_pairs={{0,1},{1,0},{2,3},{3,2},{4,5},{5,4},{6,7},{7,6},{8,9},{9,8},{10,11... | collective-permute-start | bytes 98312 | tf_op jit(solution)/shard_map/ppermute | solution.py:395
  88.2 4.2 %collective-permute-start.10 = (f32[32,256]{1,0:T(8,128)S(1)}, f32[32,256]{1,0:T(8,128)S(1)}, u32[]{:S(2)}, u32[]{:S(2)}) collective-permute-start(f32[32,256]{1,0:T(8,128)S(1)} %get-tuple-element.33), channel_id=1, source_target_pairs={{0,2},{1,3},{2,0},{3,1},{4,6},{5,7},{6,4},{7,5},{8,10},{9,11},{10,... | collective-permute-start | bytes 98312 | tf_op jit(solution)/shard_map/ppermute | solution.py:395
  89.9 4.1 %collective-permute-start.9 = (f32[32,256]{1,0:T(8,128)S(1)}, f32[32,256]{1,0:T(8,128)S(1)}, u32[]{:S(2)}, u32[]{:S(2)}) collective-permute-start(f32[32,256]{1,0:T(8,128)S(1)} %get-tuple-element.34), channel_id=1, source_target_pairs={{0,3},{1,2},{2,1},{3,0},{4,7},{5,6},{6,5},{7,4},{8,11},{9,10},{10,... | collective-permute-start | bytes 98312 | tf_op jit(solution)/shard_map/ppermute | solution.py:395
